TPU v7x, 256 devices: a whole 4x4x8 slice. The times are simulated.
256 devices in a mesh: row: 4 (over z_lo), col: 8 (over y, z_hi), head: 8 (over x, core).
Axes of the slice: x: 4, y: 4, z: 8 (z_hi: 2, z_lo: 4; z = z_hi * 4 + z_lo), core: 2. Of those that a mesh axis runs over, the one named last changes fastest.
Arguments:
- hidden_in: bfloat16 [4, 8, 384, 3072], P('row', 'col', None, 'head'), may hold values from -6 to 6
- mod_shift: float32 [3072], replicated, may hold values from -3 to 3
- mod_scale: float32 [3072], replicated, may hold values from -0.5 to 1
- mod_gate: float32 [3072], P('head'), may hold values from 0.5 to 2
- w_qkv: bfloat16 [3072, 3, 3072], P(None, None, 'head'), may hold values from -1 to 1
- query_gain: float32 [128], replicated, may hold values from 0.5 to 8
- key_gain: float32 [128], replicated, may hold values from 0.5 to 8
- w_out: bfloat16 [3072, 3072], P('head'), may hold values from -0.15625 to 0.15625
- window: int32 [4, 8, 9], P('row', 'col'), may hold values from 0 to 1, as said below
Outputs:
- hidden_out: bfloat16 [4, 8, 384, 3072], P('row', 'col', None, 'head')
Inputs may be any that keep to these rules, and one draw needn't show every extreme that they name: `window`: 0 for neighbours outside the tile grid; the centre entry is 1; other entries are 0 or 1.
All inputs are finite; a program needn't handle non-finite values.
Results may differ from a plain program's by a relative error of at most 0.018.
The roundings to bfloat16 on the way count: a program that leaves them out, or rounds other values in their place, can miss the bound.
Values may be sent and summed in bfloat16 or wider, within the bound.
A program may use at most 128 MiB of HBM per device.

v0:
```python
import jax
import jax.numpy as jnp
from jax import lax
from jax.sharding import PartitionSpec as P

HD = 128


def with_halo(cells, sides, width):
    for axis, dim in sides:
        count = lax.axis_size(axis)
        ends = count - 1
        head = lax.slice_in_dim(cells, 0, width, axis=dim)
        tail = lax.slice_in_dim(cells, cells.shape[dim] - width, cells.shape[dim], axis=dim)
        cells = jnp.concatenate(
            [
                lax.ppermute(tail, axis, [(i, (i + 1) % count) for i in range(ends)]),
                cells,
                lax.ppermute(head, axis, [((i + 1) % count, i) for i in range(ends)]),
            ],
            axis=dim,
        )
    return cells


def head_norm(values, gain):
    return values * lax.rsqrt(jnp.mean(values * values, axis=-1, keepdims=True) + 1e-06) * gain


def attend_dense(query, keys, values, valid, inverse):
    scores = jnp.einsum("qhd,jkhd->hqjk", query, keys, preferred_element_type=jnp.float32) * inverse
    scores = jnp.where(valid[None, None, :, None] > 0, scores, -1e30)
    top = jnp.max(scores, axis=(2, 3), keepdims=True)
    weights = jnp.exp(scores - top)
    total = jnp.sum(weights, axis=(2, 3), keepdims=True)
    probs = (weights / total).astype(jnp.bfloat16)
    return jnp.einsum("hqjk,jkhd->qhd", probs, values, preferred_element_type=jnp.float32).astype(
        jnp.bfloat16
    )


def on_device(
    hidden_in, mod_shift, mod_scale, mod_gate, w_qkv, query_gain, key_gain, w_out, window
):
    trows, tcols, tile, local_width = hidden_in.shape
    width = w_qkv.shape[0]
    local_heads = w_qkv.shape[2] // HD
    gathered = lax.all_gather(hidden_in, "head", axis=3, tiled=True)
    xfloat = gathered.astype(jnp.float32)
    center = jnp.mean(xfloat, axis=-1, keepdims=True)
    spread = jnp.mean((xfloat - center) ** 2, axis=-1, keepdims=True)
    normed = ((xfloat - center) * lax.rsqrt(spread + 1e-06) * (1.0 + mod_scale) + mod_shift).astype(
        jnp.bfloat16
    )
    tokens = trows * tcols * tile
    qkv = jnp.dot(
        normed.reshape(tokens, width),
        w_qkv.reshape(width, 3 * local_heads * HD),
        preferred_element_type=jnp.float32,
    )
    qkv = qkv.reshape(trows, tcols, tile, 3, local_heads, HD)
    query = head_norm(qkv[:, :, :, 0], query_gain).astype(jnp.bfloat16)
    keyed = head_norm(qkv[:, :, :, 1], key_gain).astype(jnp.bfloat16)
    valued = qkv[:, :, :, 2].astype(jnp.bfloat16)
    paired = jnp.stack([keyed, valued], axis=3).reshape(trows, tcols, tile, 2, local_heads * HD)
    padded = with_halo(paired, (("row", 0), ("col", 1)), 1)
    padded = padded.reshape(trows + 2, tcols + 2, tile, 2, local_heads, HD)
    inverse = 1.0 / jnp.sqrt(jnp.float32(HD))
    blocks = jnp.stack([padded[offset // 3, offset % 3] for offset in range(9)], axis=0)
    valid = window[0, 0]
    result = attend_dense(query[0, 0], blocks[:, :, 0], blocks[:, :, 1], valid, inverse)
    results = [result]
    attn = jnp.stack(results, axis=0).reshape(tokens, local_heads * HD)
    partial_term = jnp.dot(attn, w_out, preferred_element_type=jnp.float32)
    rounded = lax.optimization_barrier(partial_term.astype(jnp.bfloat16)).astype(jnp.float32)
    proj = lax.psum_scatter(
        rounded.reshape(trows, tcols, tile, width).astype(jnp.bfloat16),
        "head",
        scatter_dimension=3,
        tiled=True,
    ).astype(jnp.float32)
    result = hidden_in.astype(jnp.float32) + mod_gate * proj
    return result.astype(jnp.bfloat16)


def solution(mesh):
    in_specs = (
        P("row", "col", None, "head"),
        P(),
        P(),
        P("head"),
        P(None, None, "head"),
        P(),
        P(),
        P("head", None),
        P("row", "col", None),
    )
    out_specs = P("row", "col", None, "head")
    return jax.shard_map(
        on_device, mesh=mesh, in_specs=in_specs, out_specs=out_specs, check_vma=False
    )
```

profile of v0, /device:TPU:31, one launch (start us, length us, event | category | flops | bytes accessed | tf_op | source)
XLA Modules:
  0.0 345.4 jit_solution(9702555073360940547)
XLA Ops:
  7.3 10.3 %copy.34 = bf16[3072,3,384]{0,2,1:T(8,128)(2,1)} copy(bf16[3072,3,384]{2,0,1:T(8,128)(2,1)} %param.13) | data formatting | bytes 14155776 | tf_op args[4]
  17.6 21.9 %all-gather.2.cloned.1.call-done = bf16[1,1,384,3072]{3,2,1,0:T(8,128)(2,1)} async-done(((bf16[1,1,384,384]{3,2,1,0:T(8,128)(2,1)}), bf16[1,1,384,3072]{3,2,1,0:T(8,128)(2,1)}) %all-gather.2.cloned.1.call-update) | async-done | bytes 2359312 | tf_op jit(solution)/shard_map/all_gather | solution.py:48
  41.6 2.4 fusion.5
  44.0 7.1 %fusion.17 = f32[1,1,384,3,3,128]{2,5,4,3,1,0:T(8,128)S(1)} fusion(bf16[3,3,128,3072]{3,2,1,0:T(8,128)(2,1)} %bitcast.91, bf16[1,1,384,3072]{3,2,1,0:T(8,128)(2,1)} %all-gather.2.cloned.1.call-done, f32[3072]{0:T(1024)S(1)} %copy-done.11, f32[3072]{0:T(1024)S(1)} %broadcast_add_fusion, f32[384]{0:T(512)S(1)} %add_rsqrt_fusion.2, ...), kind=kOutput, calls=%fused_computation.27 | convolution fusion | flops 2724986880 | bytes 11234304 | tf_op jit(solution)/shard_map/dot_general | solution.py:56
  52.8 4.0 %collective-permute-start = (bf16[1,1,384,2,384]{2,4,3,1,0:T(8,128)(2,1)S(1)}, bf16[1,1,384,2,384]{2,4,3,1,0:T(8,128)(2,1)S(1)}, u32[]{:S(2)}, u32[]{:S(2)}) collective-permute-start(bf16[1,1,384,2,384]{2,4,3,1,0:T(8,128)(2,1)S(1)} %pad_maximum_fusion.2), channel_id=1, source_target_pairs={{0,64},{64,128},{128,192},{1,65},{65,129},{129,193},{2,66},{66,130... | collective-permute-start | bytes 1769480 | tf_op jit(solution)/shard_map/ppermute | solution.py:17
  56.9 11.2 %collective-permute-done.1 = bf16[1,1,384,2,384]{2,4,3,1,0:T(8,128)(2,1)S(1)} collective-permute-done((bf16[1,1,384,2,384]{2,4,3,1,0:T(8,128)(2,1)S(1)}, bf16[1,1,384,2,384]{2,4,3,1,0:T(8,128)(2,1)S(1)}, u32[]{:S(2)}, u32[]{:S(2)}) %collective-permute-start.1) | collective-permute-done | bytes 589856 | tf_op jit(solution)/shard_map/ppermute | solution.py:19
  69.2 7.6 %collective-permute-start.3 = (bf16[3,1,384,2,384]{2,4,3,1,0:T(8,128)(2,1)S(1)}, bf16[3,1,384,2,384]{2,4,3,1,0:T(8,128)(2,1)S(1)}, u32[]{:S(2)}, u32[]{:S(2)}) collective-permute-start(bf16[3,1,384,2,384]{2,4,3,1,0:T(8,128)(2,1)S(1)} %pad_maximum_fusion.1), channel_id=1, source_target_pairs={{8,0},{16,8},{24,16},{32,24},{40,32},{48,40},{56,48},{9,1},{17,9},... | collective-permute-start | bytes 5308424 | tf_op jit(solution)/shard_map/ppermute | solution.py:19
  79.0 35.1 %collective-permute-done.3 = bf16[3,1,384,2,384]{2,4,3,1,0:T(8,128)(2,1)S(1)} collective-permute-done((bf16[3,1,384,2,384]{2,4,3,1,0:T(8,128)(2,1)S(1)}, bf16[3,1,384,2,384]{2,4,3,1,0:T(8,128)(2,1)S(1)}, u32[]{:S(2)}, u32[]{:S(2)}) %collective-permute-start.3) | collective-permute-done | bytes 1769504 | tf_op jit(solution)/shard_map/ppermute | solution.py:19
  114.0 75.2 %collective-permute-done.2 = bf16[3,1,384,2,384]{2,4,3,1,0:T(8,128)(2,1)S(1)} collective-permute-done((bf16[3,1,384,2,384]{2,4,3,1,0:T(8,128)(2,1)S(1)}, bf16[3,1,384,2,384]{2,4,3,1,0:T(8,128)(2,1)S(1)}, u32[]{:S(2)}, u32[]{:S(2)}) %collective-permute-start.2) | collective-permute-done | bytes 1769504 | tf_op jit(solution)/shard_map/ppermute | solution.py:17
  190.0 2.2 fusion.30
  193.9 2.1 copy.63
  196.1 2.1 copy.62
  198.2 2.1 copy.61
  200.3 2.1 copy.60
  202.5 2.1 copy.59
  204.6 2.1 copy.58
  206.7 2.1 copy.57
  215.0 8.3 %fusion = (f32[3,384]{1,0:T(4,128)S(1)}, f32[3,384,9,384]{1,3,2,0:T(8,128)}) fusion(pred[9]{0:T(512)(128)(4,1)S(1)} %compare_bitcast_fusion, bf16[9,384,2,3,128]{4,1,0,3,2:T(8,128)(2,1)S(1)} %bitcast_dynamic-update-slice_fusion, f32[1,1,384,3,3,128]{2,5,4,3,1,0:T(8,128)} %copy-done.1, f32[128]{0:T(128)S(1)} %copy-done.8, f32[384,3]{0,1:T(4,128)S(1)} %get-tuple-element.18), kind=kOutput, calls=%fused_computation.3 | convolution fusion | flops 1031601024 | bytes 19181056 | tf_op jit(solution)/shard_map/qhd,jkhd->hqjk/dot_general | solution.py:31
  223.3 8.9 %fusion.1 = f32[3,384]{1,0:T(4,128)S(1)} fusion(f32[3,384,9,384]{1,3,2,0:T(8,128)} %get-tuple-element.17, f32[3,384]{1,0:T(4,128)S(1)} %get-tuple-element.16, pred[9]{0:T(512)(128)(4,1)S(1)} %compare_bitcast_fusion), kind=kLoop, calls=%fused_computation.4 | loop fusion | flops 15924096 | bytes 15934473 | tf_op jit(solution)/shard_map/reduce_sum | solution.py:35
  232.2 7.9 %fusion.21 = bf16[3,128,384]{2,1,0:T(8,128)(2,1)S(1)} fusion(f32[3,384,9,384]{1,3,2,0:T(8,128)} %get-tuple-element.17, f32[3,384]{1,0:T(4,128)S(1)} %fusion.1, f32[3,384]{1,0:T(4,128)S(1)} %get-tuple-element.16, pred[9]{0:T(512)(128)(4,1)S(1)} %compare_bitcast_fusion, bf16[9,384,2,3,128]{4,1,0,3,2:T(8,128)(2,1)S(1)} %copy-done.5), kind=kOutput, calls=%fused_computation.29 | convolution fusion | flops 1039269888 | bytes 18887168 | tf_op jit(solution)/shard_map/hqjk,jkhd->qhd/dot_general | solution.py:37
  240.1 2.9 convolution_convert_fusion
  242.9 10.8 %copy.54 = bf16[1,1,384,3072]{2,1,0,3:T(2,128)(2,1)} copy(bf16[1,1,384,3072]{3,2,1,0:T(8,128)(2,1)} %bitcast.90) | data formatting | bytes 4718592
  253.7 4.2 %copy.67 = bf16[3072,1,1,384]{3,0,1,2:T(8,128)(2,1)} copy(bf16[3072,1,1,384]{3,2,1,0:T(2,128)(2,1)} %bitcast.88) | data formatting | bytes 4718592
  257.9 77.7 %reduce-scatter.4.cloned.1.call-done = bf16[384,384]{1,0:T(8,128)(2,1)} async-done(((bf16[3072,384]{1,0:T(8,128)(2,1)}), bf16[384,384]{1,0:T(8,128)(2,1)}) %reduce-scatter.4.cloned.1.call-update) | async-done | bytes 294928
  (59 shorter events, 19.2 us)
Async XLA Ops:
  6.5 233.5 %copy-start = (bf16[384,3072]{1,0:T(8,128)(2,1)S(1)}, bf16[384,3072]{1,0:T(8,128)(2,1)}, u32[]{:S(2)}) copy-start(bf16[384,3072]{1,0:T(8,128)(2,1)} %param.16) | copy-start | bytes 7077892
  6.5 33.0 %all-gather.2.cloned.1.call-start = ((), (), s32[]{:S(2)}) async-start(), calls=%async_computation.1 | async-start | bytes 2654208 | tf_op jit(solution)/shard_map/all_gather | solution.py:48
  7.3 10.4 %copy-start.7 = (f32[3072]{0:T(1024)S(1)}, f32[3072]{0:T(1024)}, u32[]{:S(2)}) copy-start(f32[3072]{0:T(1024)} %param.11) | copy-start | bytes 36868
  7.3 36.7 %copy-start.11 = (f32[3072]{0:T(1024)S(1)}, f32[3072]{0:T(1024)}, u32[]{:S(2)}) copy-start(f32[3072]{0:T(1024)} %param.10) | copy-start | bytes 36868
  7.3 328.4 %reduce-scatter.4.cloned.1.call-start = ((), (), s32[]{:S(2)}) async-start(), calls=%async_computation.2 | async-start | bytes 2654208
  44.0 7.3 %copy-start.10 = (f32[128]{0:T(128)S(1)}, f32[128]{0:T(128)}, u32[]{:S(2)}) copy-start(f32[128]{0:T(128)} %param.15) | copy-start | bytes 1540
  51.1 138.9 %copy-start.1 = (f32[1,1,384,3,3,128]{2,5,4,3,1,0:T(8,128)}, f32[1,1,384,3,3,128]{2,5,4,3,1,0:T(8,128)S(1)}, u32[]{:S(2)}) copy-start(f32[1,1,384,3,3,128]{2,5,4,3,1,0:T(8,128)S(1)} %fusion.17) | copy-start | bytes 5308420
  51.2 27.8 %copy-start.12 = (s32[1,1,9]{2,1,0:T(1,128)S(1)}, s32[1,1,9]{2,1,0:T(1,128)}, u32[]{:S(2)}) copy-start(s32[1,1,9]{2,1,0:T(1,128)} %param.17) | copy-start | bytes 112
  51.5 16.5 %collective-permute-start.1 = (bf16[1,1,384,2,384]{2,4,3,1,0:T(8,128)(2,1)S(1)}, bf16[1,1,384,2,384]{2,4,3,1,0:T(8,128)(2,1)S(1)}, u32[]{:S(2)}, u32[]{:S(2)}) collective-permute-start(bf16[1,1,384,2,384]{2,4,3,1,0:T(8,128)(2,1)S(1)} %pad_maximum_fusion.2), channel_id=1, source_target_pairs={{64,0},{128,64},{192,128},{65,1},{129,65},{193,129},{66,2},{130,66... | collective-permute-start | bytes 1769480 | tf_op jit(solution)/shard_map/ppermute | solution.py:19
  52.8 16.1 %collective-permute-start = (bf16[1,1,384,2,384]{2,4,3,1,0:T(8,128)(2,1)S(1)}, bf16[1,1,384,2,384]{2,4,3,1,0:T(8,128)(2,1)S(1)}, u32[]{:S(2)}, u32[]{:S(2)}) collective-permute-start(bf16[1,1,384,2,384]{2,4,3,1,0:T(8,128)(2,1)S(1)} %pad_maximum_fusion.2), channel_id=1, source_target_pairs={{0,64},{64,128},{128,192},{1,65},{65,129},{129,193},{2,66},{66,130... | collective-permute-start | bytes 1769480 | tf_op jit(solution)/shard_map/ppermute | solution.py:17
  69.2 44.8 %collective-permute-start.3 = (bf16[3,1,384,2,384]{2,4,3,1,0:T(8,128)(2,1)S(1)}, bf16[3,1,384,2,384]{2,4,3,1,0:T(8,128)(2,1)S(1)}, u32[]{:S(2)}, u32[]{:S(2)}) collective-permute-start(bf16[3,1,384,2,384]{2,4,3,1,0:T(8,128)(2,1)S(1)} %pad_maximum_fusion.1), channel_id=1, source_target_pairs={{8,0},{16,8},{24,16},{32,24},{40,32},{48,40},{56,48},{9,1},{17,9},... | collective-permute-start | bytes 5308424 | tf_op jit(solution)/shard_map/ppermute | solution.py:19
  76.8 112.4 %collective-permute-start.2 = (bf16[3,1,384,2,384]{2,4,3,1,0:T(8,128)(2,1)S(1)}, bf16[3,1,384,2,384]{2,4,3,1,0:T(8,128)(2,1)S(1)}, u32[]{:S(2)}, u32[]{:S(2)}) collective-permute-start(bf16[3,1,384,2,384]{2,4,3,1,0:T(8,128)(2,1)S(1)} %pad_maximum_fusion.1), channel_id=1, source_target_pairs={{0,8},{8,16},{16,24},{24,32},{32,40},{40,48},{48,56},{1,9},{9,17},... | collective-permute-start | bytes 5308424 | tf_op jit(solution)/shard_map/ppermute | solution.py:17
  208.8 5.8 %copy-start.3 = (bf16[1,1,384,2,3,128]{5,2,4,3,1,0:T(8,128)(2,1)S(1)}, bf16[1,1,384,2,3,128]{5,2,4,3,1,0:T(8,128)(2,1)}, u32[]{:S(2)}) copy-start(bf16[1,1,384,2,3,128]{5,2,4,3,1,0:T(8,128)(2,1)} %copy.62) | copy-start | bytes 1769476
  208.8 5.9 %copy-start.2 = (bf16[1,1,384,2,3,128]{5,2,4,3,1,0:T(8,128)(2,1)S(1)}, bf16[1,1,384,2,3,128]{5,2,4,3,1,0:T(8,128)(2,1)}, u32[]{:S(2)}) copy-start(bf16[1,1,384,2,3,128]{5,2,4,3,1,0:T(8,128)(2,1)} %copy.63) | copy-start | bytes 1769476
  208.8 6.2 %copy-start.8 = (f32[128]{0:T(128)S(1)}, f32[128]{0:T(128)}, u32[]{:S(2)}) copy-start(f32[128]{0:T(128)} %param.14) | copy-start | bytes 1540
  215.0 8.3 %copy-start.4 = (bf16[9,384,2,3,128]{4,1,0,3,2:T(8,128)(2,1)}, bf16[9,384,2,3,128]{4,1,0,3,2:T(8,128)(2,1)S(1)}, u32[]{:S(2)}) copy-start(bf16[9,384,2,3,128]{4,1,0,3,2:T(8,128)(2,1)S(1)} %bitcast_dynamic-update-slice_fusion) | copy-start | bytes 15925252
  223.3 8.9 %copy-start.5 = (bf16[9,384,2,3,128]{4,1,0,3,2:T(8,128)(2,1)S(1)}, bf16[9,384,2,3,128]{4,1,0,3,2:T(8,128)(2,1)}, u32[]{:S(2)}) copy-start(bf16[9,384,2,3,128]{4,1,0,3,2:T(8,128)(2,1)} %copy-done.4) | copy-start | bytes 15925252
  253.7 84.1 %copy-start.6 = (bf16[1,1,384,384]{3,2,1,0:T(8,128)(2,1)S(1)}, bf16[1,1,384,384]{3,2,1,0:T(8,128)(2,1)}, u32[]{:S(2)}) copy-start(bf16[1,1,384,384]{3,2,1,0:T(8,128)(2,1)} %param.9) | copy-start | bytes 884740
  253.7 84.1 %copy-start.9 = (f32[384]{0:T(512)S(1)}, f32[384]{0:T(512)}, u32[]{:S(2)}) copy-start(f32[384]{0:T(512)} %param.12) | copy-start | bytes 4612
Sparse Core Ops, SparseCore 0:
  9.2 30.2 all-gather.1
  258.1 77.5 reduce-scatter.3
where the time goes:
time: 349 us; the launch traced here: 345 us
  waiting for transfers between devices  223 us (64%)
  local copies, waits for them, and re-layouts  52.4 us (15%)
  matrix products  26.2 us (8%)
  other arithmetic  15.5 us (4%)
  starting transfers between devices  15.1 us (4%)
  between operations  13.7 us (4%)
    unnamed x3, waiting for transfers between devices  78.4 us
    ppermute x2, waiting for transfers between devices, with_halo(): lax.ppermute(tail, axis, [(i, (i + 1) % count) for i in range(ends)])  76.1 us
    unnamed x48, local copies, waits for them, and re-layouts  50 us
    ppermute x2, waiting for transfers between devices, with_halo(): lax.ppermute(head, axis, [((i + 1) % count, i) for i in range(ends)])  46.3 us
    all_gather x1, waiting for transfers between devices, on_device(): gathered = lax.all_gather(hidden_in, 'head', axis=3, tiled=True)  21.9 us
    ppermute x2, starting transfers between devices, with_halo(): lax.ppermute(head, axis, [((i + 1) % count, i) for i in range(ends)])  8.93 us
    reduce_sum x1, other arithmetic, attend_dense(): total = jnp.sum(weights, axis=(2, 3), keepdims=True)  8.86 us
    dot_general x1, matrix products, attend_dense(): jnp.einsum('qhd,jkhd->hqjk', query, keys, preferred_element_type=jnp.floa...  8.29 us
  transfers between devices with their start and end apart: 6, of which 6 were waited for; matrix products, arithmetic and copies ran while one was open for 3% of the time, Pallas kernels for 0%

commit v1 on v0

v1 whole, which is shorter than its diff:
```python
import functools
import math

import jax
import jax.numpy as jnp
from jax import lax
from jax.experimental import pallas as pl
from jax.experimental.pallas import tpu as pltpu
from jax.sharding import PartitionSpec as P

MESH = pl.DeviceIdType.MESH
F32 = jnp.float32
BF16 = jnp.bfloat16
HD = 128
NH = 3
NG = 8
T = 384
W = NH * HD
D = NG * W
ROWS = 4
OWN, BELOW, ABOVE, FAR = 4, 5, 6, 7
SLOTS = 10
SCALE = math.log2(math.e) / math.sqrt(HD)
NEG = -1e30
LAG = 3


def kernel(
    x_ref, shift_ref, scale_ref, gate_ref, w_hbm, qg_ref, kg_ref, wo_hbm, win_ref, out_ref,
    hg, nb, wq, kv, qs, acc, m_s, l_s, wo, at,
    w_sem, own_sem, ag_s, agf_s, ag_r, kv_s, y_s, kv_r, wo_s, wo_r, at_s, atf_s, at_r,
):
    r = lax.axis_index("row")
    c = lax.axis_index("col")
    g = lax.axis_index("head")
    y, zh = c // 2, c % 2
    core = g % 2
    mate = g + 1 - 2 * core
    peers = [lax.rem(g + 2, NG), lax.rem(g + 6, NG), lax.rem(g + 4, NG)]
    z_next = (jnp.where(r < 3, r + 1, 0), jnp.where(r < 3, c, c + 1 - 2 * zh), g)
    z_prev = (jnp.where(r > 0, r - 1, 3), jnp.where(r > 0, c, c + 1 - 2 * zh), g)
    y_next = (r, lax.rem(c + 2, 8), g)
    y_prev = (r, lax.rem(c + 6, 8), g)
    y_out = (r, lax.rem(jnp.where(zh == 0, c + 2, c + 6), 8), g)
    has_out = jnp.where(zh == 0, y < 3, y > 0)
    has_in = jnp.where(zh == 0, y > 0, y < 3)

    def on_head(i):
        return (r, c, i)

    w_copies = [pltpu.make_async_copy(w_hbm.at[j], wq.at[j], w_sem.at[j]) for j in range(3)]
    for j in (1, 2, 0):
        w_copies[j].start()

    def columns(i):
        return wo_hbm.at[:, pl.ds(pl.multiple_of(i * W, W), W)]

    wo_own = pltpu.make_async_copy(columns(g), wo.at[g], own_sem)
    wo_own.start()

    barrier = pltpu.get_barrier_semaphore()
    for i in range(1, NG):
        pl.semaphore_signal(barrier, inc=1, device_id=on_head(lax.rem(g + i, NG)), device_id_type=MESH)
    for dev in (z_next, z_prev, y_next, y_prev):
        pl.semaphore_signal(barrier, inc=1, device_id=dev, device_id_type=MESH)
    pl.semaphore_wait(barrier, NG - 1 + 4)

    def ag_copy(src, slot, send, dev):
        return pltpu.make_async_remote_copy(
            src_ref=src, dst_ref=hg.at[slot], send_sem=send, recv_sem=ag_r.at[slot],
            device_id=on_head(dev), device_id_type=MESH)

    firsts = [ag_copy(x_ref, g, ag_s.at[i], dev) for i, dev in enumerate(peers + [mate])]
    for copy in firsts:
        copy.start()
    hg[g] = x_ref[...]
    forwards = []
    for i, dev in enumerate(peers):
        ag_copy(x_ref, dev, ag_s.at[i], dev).wait_recv()
        forward = ag_copy(hg.at[dev], dev, agf_s.at[i], mate)
        forward.start()
        forwards.append(forward)
    ag_copy(x_ref, mate, ag_s.at[3], mate).wait_recv()
    for i, dev in enumerate(peers):
        other = dev + 1 - 2 * core
        ag_copy(x_ref, other, agf_s.at[i], mate).wait_recv()

    step = 32

    def norm_rows(i, _):
        rows = pl.ds(pl.multiple_of(i * step, step), step)
        parts = [hg[j, rows, :].astype(F32) for j in range(NG)]
        total = parts[0]
        for part in parts[1:]:
            total = total + part
        center = jnp.sum(total, axis=-1, keepdims=True) * (1.0 / D)
        squares = None
        for part in parts:
            off = part - center
            squares = off * off if squares is None else squares + off * off
        spread = jnp.sum(squares, axis=-1, keepdims=True) * (1.0 / D)
        inv = lax.rsqrt(spread + 1e-6)
        for j in range(NG):
            cols = slice(j * W, (j + 1) * W)
            nb[rows, cols] = (
                (parts[j] - center) * inv * (1.0 + scale_ref[:, cols]) + shift_ref[:, cols]
            ).astype(BF16)
        return 0

    lax.fori_loop(0, T // step, norm_rows, 0)

    def kv_copy(src, dst, h, part, send, dev):
        return pltpu.make_async_remote_copy(
            src_ref=kv.at[src, h, part], dst_ref=kv.at[dst, h, part],
            send_sem=send, recv_sem=kv_r.at[dst, h, part],
            device_id=dev, device_id_type=MESH)

    def send_own(h, part):
        kv_copy(OWN, jnp.where(r == 0, 0, BELOW), h, part, kv_s.at[0, 0, h, part], z_prev).start()
        kv_copy(OWN, jnp.where(r == 3, 3, ABOVE), h, part, kv_s.at[1, 0, h, part], z_next).start()

    def project(j):
        w_copies[j].wait()
        return jnp.dot(nb[...], wq[j], preferred_element_type=F32)

    def head_norm(values, gain):
        mean = jnp.mean(values * values, axis=-1, keepdims=True)
        return (values * lax.rsqrt(mean + 1e-6) * gain).astype(BF16)

    keys = project(1)
    for h in range(NH):
        kv[OWN, h, 0] = head_norm(keys[:, h * HD:(h + 1) * HD], kg_ref[...])
        send_own(h, 0)
    values = project(2)
    for h in range(NH):
        kv[OWN, h, 1] = values[:, h * HD:(h + 1) * HD].astype(BF16)
        send_own(h, 1)
    queries = project(0)
    for h in range(NH):
        qs[h] = head_norm(queries[:, h * HD:(h + 1) * HD], qg_ref[...])

    def wo_copy(i):
        dev = lax.rem(g + i, NG)
        return pltpu.make_async_remote_copy(
            src_ref=columns(dev), dst_ref=wo.at[g], send_sem=wo_s.at[i], recv_sem=wo_r.at[g],
            device_id=on_head(dev), device_id_type=MESH)

    for i in range(1, NG):
        wo_copy(i).start()

    m_s[...] = jnp.full_like(m_s, NEG)
    l_s[...] = jnp.zeros_like(l_s)
    acc[...] = jnp.zeros_like(acc)
    block = 128

    def attend(slot, h, offset):
        kept = win_ref[offset] > 0
        k = kv[slot, h, 0]
        v = kv[slot, h, 1]
        for i in range(T // block):
            rows = slice(i * block, (i + 1) * block)
            s = lax.dot_general(
                qs[h, rows, :], k, (((1,), (1,)), ((), ())), preferred_element_type=F32)
            top = jnp.max(s, axis=-1, keepdims=True) * SCALE
            old = m_s[h, rows, :]
            new = jnp.maximum(old, jnp.where(kept, top, NEG))
            decay = jnp.exp2(old - new)
            less = jnp.where(kept, new, -NEG)
            p = jnp.exp2(s * SCALE - jnp.concatenate([less] * (T // HD), axis=1))
            m_s[h, rows, :] = new
            l_s[h, rows, :] = l_s[h, rows, :] * decay + jnp.sum(p, axis=-1, keepdims=True)
            acc[h, rows, :] = acc[h, rows, :] * decay + jnp.dot(
                p.astype(BF16), v, preferred_element_type=F32)

    def own_tile(h, _):
        attend(OWN, h, 4)
        return 0

    lax.fori_loop(0, NH, own_tile, 0)

    def arrived(slot, h, part):
        kv_copy(OWN, slot, h, part, kv_s.at[0, 0, h, part], z_prev).wait_recv()

    near = jnp.where(r >= 2, 0, 1)
    lag = jnp.where((r == 0) | (r == 3), LAG, 1)

    def x_slot(stream, e):
        return jnp.where(stream == 0, e // NH, 3 - e // NH)

    def inside(slot):
        return (slot >= r - 1) & (slot <= r + 1)

    def x_event(stream, e):
        slot, h, k = x_slot(stream, e), lax.rem(e, NH), e // NH
        for part in range(2):
            arrived(slot, h, part)

            @pl.when((stream == 0) & (r > 0))
            def _():
                kv_copy(slot, slot, h, part, kv_s.at[0, 1 + k, h, part], z_prev).start()

            @pl.when((stream == 1) & (r < 3))
            def _():
                kv_copy(slot, slot, h, part, kv_s.at[1, 1 + k, h, part], z_next).start()

            @pl.when(inside(slot) & has_out)
            def _():
                turn = slot - r + 1
                kv_copy(slot, FAR + turn, h, part, y_s.at[turn, h, part], y_out).start()

    def valid_event(e):
        return (e >= 0) & (e < 2 * NH)

    def at_copy(slot, h, send, dev):
        return pltpu.make_async_remote_copy(
            src_ref=at.at[slot, h], dst_ref=at.at[slot, h], send_sem=send, recv_sem=at_r.at[slot, h],
            device_id=on_head(dev), device_id_type=MESH)

    def finish_head(h):
        at[g, h] = (acc[h] / l_s[h]).astype(BF16)
        for i, dev in enumerate(peers + [mate]):
            at_copy(g, h, at_s.at[i, h], dev).start()

    def pass_head(h):
        for i, dev in enumerate(peers):
            at_copy(dev, h, at_s.at[i, h], dev).wait_recv()
            at_copy(dev, h, atf_s.at[i, h], mate).start()

    def tick(t, _):
        @pl.when(t < NH)
        def _():
            @pl.when(r < 3)
            def _():
                for part in range(2):
                    arrived(BELOW, t, part)

                    @pl.when(r == 0)
                    def _():
                        kv_copy(BELOW, 1, t, part, kv_s.at[0, 1, t, part], z_prev).start()

            @pl.when(r > 0)
            def _():
                for part in range(2):
                    arrived(ABOVE, t, part)

                    @pl.when(r == 3)
                    def _():
                        kv_copy(ABOVE, 2, t, part, kv_s.at[1, 1, t, part], z_next).start()

        e_near, e_far = t, t - lag

        @pl.when(valid_event(e_near))
        def _():
            x_event(near, e_near)

        @pl.when(valid_event(e_far))
        def _():
            x_event(1 - near, e_far)

        def compute(i, _):
            stream = jnp.where(lax.rem(i, 2) == 0, near, 1 - near)
            e = jnp.where(lax.rem(i, 2) == 0, t, t - lag) - jnp.where(i >= 4, 1, 0)
            e_ok = valid_event(e)
            e = jnp.where(e_ok, e, 0)
            slot_x = x_slot(stream, e)
            turn = slot_x - r + 1
            is_far = i >= 4
            slot = jnp.where(
                i < 2, jnp.where(i == 0, BELOW, ABOVE), jnp.where(is_far, FAR + turn, slot_x))
            h = jnp.where(i < 2, t, lax.rem(e, NH))
            ok = jnp.where(
                i < 2,
                (t < NH) & jnp.where(i == 0, r < 3, r > 0),
                e_ok & inside(slot_x) & (jnp.logical_not(is_far) | has_in))
            side = jnp.where(is_far, 2 * zh, 2 - 2 * zh)
            offset = jnp.where(i < 2, jnp.where(i == 0, 7, 1), 3 * turn + side)

            @pl.when(ok)
            def _():
                @pl.when(is_far)
                def _():
                    arrived(slot, h, 0)
                    arrived(slot, h, 1)

                attend(slot, h, offset)

            return 0

        lax.fori_loop(0, 6, compute, 0)
        done = t - lag - NH - 1

        @pl.when((done >= 0) & (done < NH))
        def _():
            finish_head(done)

            @pl.when(done > 0)
            def _():
                pass_head(done - 1)

        return 0

    lax.fori_loop(0, 2 * NH + LAG + 1, tick, 0)
    pass_head(NH - 1)
    for h in range(NH):
        at_copy(mate, h, at_s.at[3, h], mate).wait_recv()
        for i, dev in enumerate(peers):
            at_copy(dev + 1 - 2 * core, h, atf_s.at[i, h], mate).wait_recv()
    wo_own.wait()
    for i in range(1, NG):
        src = lax.rem(g + i, NG)
        pltpu.make_async_remote_copy(
            src_ref=columns(src), dst_ref=wo.at[src], send_sem=wo_s.at[i], recv_sem=wo_r.at[src],
            device_id=on_head(src), device_id_type=MESH).wait_recv()


    def group(i, total):
        a = jnp.concatenate([at[i, h] for h in range(NH)], axis=1)
        part = jnp.dot(a, wo[i], preferred_element_type=F32)
        return total + part.astype(BF16).astype(F32)

    proj = lax.fori_loop(0, NG, group, jnp.zeros((T, W), F32))
    out_ref[...] = (x_ref[...].astype(F32) + gate_ref[...] * proj).astype(BF16)

    for copy in firsts + forwards:
        copy.wait_send()
    for i in range(1, NG):
        wo_copy(i).wait_send()
    for h in range(NH):
        for i, dev in enumerate(peers + [mate]):
            at_copy(g, h, at_s.at[i, h], dev).wait_send()
        for i, dev in enumerate(peers):
            at_copy(dev, h, atf_s.at[i, h], mate).wait_send()

    def sent(i, _):
        h, part = i // 2, lax.rem(i, 2)
        for k in range(3):
            @pl.when((r > 0) | (k < 2))
            def _():
                kv_copy(OWN, OWN, h, part, kv_s.at[0, k, h, part], z_prev).wait_send()

            @pl.when((r < 3) | (k < 2))
            def _():
                kv_copy(OWN, OWN, h, part, kv_s.at[1, k, h, part], z_next).wait_send()

            j = r - 1 + k

            @pl.when(has_out & (j >= 0) & (j < ROWS))
            def _():
                kv_copy(OWN, OWN, h, part, y_s.at[k, h, part], y_out).wait_send()

        return 0

    lax.fori_loop(0, 2 * NH, sent, 0)


def on_device(
    hidden_in, mod_shift, mod_scale, mod_gate, w_qkv, query_gain, key_gain, w_out, window
):
    vmem = pl.BlockSpec(memory_space=pltpu.VMEM)
    hbm = pl.BlockSpec(memory_space=pl.ANY)
    smem = pl.BlockSpec(memory_space=pltpu.SMEM)
    dma = pltpu.SemaphoreType.DMA
    out = pl.pallas_call(
        kernel,
        out_shape=jax.ShapeDtypeStruct((T, W), BF16),
        in_specs=[vmem, vmem, vmem, vmem, hbm, vmem, vmem, hbm, smem],
        out_specs=vmem,
        scratch_shapes=[
            pltpu.VMEM((NG, T, W), BF16),
            pltpu.VMEM((T, D), BF16),
            pltpu.VMEM((3, D, W), BF16),
            pltpu.VMEM((SLOTS, NH, 2, T, HD), BF16),
            pltpu.VMEM((NH, T, HD), BF16),
            pltpu.VMEM((NH, T, HD), F32),
            pltpu.VMEM((NH, T, HD), F32),
            pltpu.VMEM((NH, T, HD), F32),
            pltpu.VMEM((NG, W, W), BF16),
            pltpu.VMEM((NG, NH, T, HD), BF16),
            dma((3,)), dma, dma((4,)), dma((3,)), dma((NG,)),
            dma((2, 3, NH, 2)), dma((3, NH, 2)), dma((SLOTS, NH, 2)),
            dma((NG,)), dma((NG,)), dma((4, NH)), dma((3, NH)), dma((NG, NH)),
        ],
        compiler_params=pltpu.CompilerParams(
            collective_id=0, has_side_effects=True, vmem_limit_bytes=48 * 1024 * 1024),
        cost_estimate=pl.CostEstimate(
            flops=6_000_000_000, bytes_accessed=10_000_000, transcendentals=4_000_000),
        name="tile_attention",
    )(
        hidden_in.reshape(T, W),
        mod_shift.reshape(1, D),
        mod_scale.reshape(1, D),
        mod_gate.reshape(1, W),
        jnp.transpose(w_qkv, (1, 0, 2)),
        query_gain.reshape(1, HD),
        key_gain.reshape(1, HD),
        w_out,
        window.reshape(9),
    )
    return out.reshape(hidden_in.shape)


def solution(mesh):
    in_specs = (
        P("row", "col", None, "head"),
        P(),
        P(),
        P("head"),
        P(None, None, "head"),
        P(),
        P(),
        P("head", None),
        P("row", "col", None),
    )
    out_specs = P("row", "col", None, "head")
    return jax.shard_map(
        on_device, mesh=mesh, in_specs=in_specs, out_specs=out_specs, check_vma=False
    )
```

time: 349 us -> 111 us (0.32)
  waiting for transfers between devices: 223 us -> 0 us
  Pallas kernels: 0 us -> 102 us
  local copies, waits for them, and re-layouts: 52.4 us -> 7.4 us
  matrix products: 26.2 us -> 0 us
  other arithmetic: 15.5 us -> 0 us
  starting transfers between devices: 15.1 us -> 0 us
  between operations: 13.7 us -> 0.02 us
    ppermute x4 -> x0, waiting for transfers between devices: 122 us -> none  [the longest x2 76.1 us: with_halo(): lax.ppermute(tail, axis, [(i, (i + 1) % count) for i in range(ends)])]
    pallas_call x0 -> x1, Pallas kernels: none -> 102 us  [on_device(): pl.pallas_call(kernel, out_shape=jax.ShapeDtypeStruct((T, W), BF16), in_s...]
    unnamed x3 -> x0, waiting for transfers between devices: 78.4 us -> none
    unnamed x48 -> x15, local copies, waits for them, and re-layouts: 50 us -> 6.72 us
    dot_general x4 -> x0, matrix products: 26.2 us -> none  [the longest x1 8.29 us: attend_dense(): jnp.einsum('qhd,jkhd->hqjk', query, keys, preferred_element_type=jnp.floa...]
    all_gather x1 -> x0, waiting for transfers between devices: 21.9 us -> none  [on_device(): gathered = lax.all_gather(hidden_in, 'head', axis=3, tiled=True)]
    ppermute x4 -> x0, starting transfers between devices: 15.1 us -> none  [the longest x2 8.93 us: with_halo(): lax.ppermute(head, axis, [((i + 1) % count, i) for i in range(ends)])]
    reduce_sum x4 -> x0, other arithmetic: 13.4 us -> none  [the longest x1 8.86 us: attend_dense(): total = jnp.sum(weights, axis=(2, 3), keepdims=True)]
  transfers between devices with their start and end apart: 6 -> 0, of which waited for: 6 -> 0; matrix products, arithmetic and copies ran while one was open for 3% -> 0% of each run, Pallas kernels for 0% -> 0%
where the time goes in v1:
time: 111 us; the launch traced here: 109 us
  Pallas kernels  102 us (92%)
  local copies, waits for them, and re-layouts  7.4 us (7%)
    pallas_call x1, Pallas kernels, on_device(): pl.pallas_call(kernel, out_shape=jax.ShapeDtypeStruct((T, W), BF16), in_s...  102 us
    unnamed x15, local copies, waits for them, and re-layouts  6.72 us

profile of v1, /device:TPU:31, one launch (start us, length us, event | category | flops | bytes accessed | tf_op | source)
XLA Modules:
  0.0 109.5 jit_solution(10137164042306529169)
XLA Ops:
  0.0 0.7 reshape.27.gate_ref
  0.7 0.0 copy-start
  0.7 1.7 %copy-done = bf16[384,3072]{1,0:T(8,128)(2,1)S(1)} copy-done((bf16[384,3072]{1,0:T(8,128)(2,1)S(1)}, bf16[384,3072]{1,0:T(8,128)(2,1)}, u32[]{:S(2)}) %copy-start) | copy-done | bytes 2359320
  2.3 0.0 copy-start.1
  2.4 1.0 copy-done.1
  3.3 0.0 copy-start.2
  3.3 0.7 copy-done.2
  4.0 0.0 copy-start.3
  4.0 0.7 copy-done.3
  4.7 0.0 copy-start.4
  4.7 0.7 copy-done.4
  5.4 0.0 copy-start.5
  5.4 0.7 copy-done.5
  6.0 0.0 copy-start.6
  6.0 0.7 copy-done.6
  6.7 102.0 %tile_attention.1 = bf16[384,384]{1,0:T(8,128)(2,1)S(1)} custom-call(bf16[384,384]{1,0:T(8,128)(2,1)S(1)} %bitcast.9, f32[1,3072]{1,0:T(1,128)S(1)} %bitcast.10, f32[1,3072]{1,0:T(1,128)S(1)} %bitcast.11, f32[1,384]{1,0:T(1,128)S(1)} %reshape.27.gate_ref, bf16[3,3072,384]{2,1,0:T(8,128)(2,1)} %bitcast.15, f32[1,128]{1,0:T(1,128)S(1)} %bitcast.12, ...), custom_call_target="tpu_custom_call" | custom-call | flops 6000000000 | bytes 10000000 | tf_op jit(solution)/shard_map/tile_attention/pallas_call | solution.py:363
  108.7 0.7 copy.11
Async XLA Ops:
  0.7 1.7 %copy-start = (bf16[384,3072]{1,0:T(8,128)(2,1)S(1)}, bf16[384,3072]{1,0:T(8,128)(2,1)}, u32[]{:S(2)}) copy-start(bf16[384,3072]{1,0:T(8,128)(2,1)} %wo_hbm.1) | copy-start | bytes 7077892
  2.3 1.0 copy-start.1
  3.3 0.7 copy-start.2
  4.0 0.7 copy-start.3
  4.7 0.7 copy-start.4
  5.4 0.7 copy-start.5
  6.0 0.7 copy-start.6

commit v2 on v1

v2 whole, which is shorter than its diff:
```python
import functools
import math

import jax
import jax.numpy as jnp
from jax import lax
from jax.experimental import pallas as pl
from jax.experimental.pallas import tpu as pltpu
from jax.sharding import PartitionSpec as P

MESH = pl.DeviceIdType.MESH
F32 = jnp.float32
BF16 = jnp.bfloat16
HD = 128
NH = 3
NG = 8
T = 384
W = NH * HD
D = NG * W
ROWS = 4
OWN, MATE = 6, 7
SLOTS = 10
SCALE = math.log2(math.e) / math.sqrt(HD)
NEG = -1e30
EVENTS = 9
LAG_OWN, LAG = 1, 2
LAG_BACK = 1


def kernel(
    x_hbm, shift_hbm, scale_hbm, w_hbm, qg_hbm, kg_hbm, wo_hbm, win_hbm, out_ref,
    shift_ref, scale_ref, qg_ref, kg_ref, win_ref, small_sem, hg, nb, wq, kv, qs, acc, m_s, l_s, wo, at, mk, back, stats,
    w_sem, own_sem, ag_s, agx_s, agf_s, ag_r, kv_s, z_s, mate_s, kv_r, q_s, q_r, mk_s, mk_r, back_s, back_r, wo_s, wo_r, at_s, atf_s, at_r,
):
    r = lax.axis_index("row")
    c = lax.axis_index("col")
    g = lax.axis_index("head")
    y, zh = c // 2, c % 2
    core = g % 2
    mate = g + 1 - 2 * core
    right, left = lax.rem(g + 2, NG), lax.rem(g + 6, NG)
    peers = [lax.rem(g + 2, NG), lax.rem(g + 6, NG), lax.rem(g + 4, NG)]
    x0 = g - core
    z_next = (jnp.where(r < 3, r + 1, 0), jnp.where(r < 3, c, c + 1 - 2 * zh))
    z_prev = (jnp.where(r > 0, r - 1, 3), jnp.where(r > 0, c, c + 1 - 2 * zh))
    rank = jnp.where(core == 0, r, 3 - r)
    onward = (
        jnp.where(core == 0, z_prev[0], z_next[0]), jnp.where(core == 0, z_prev[1], z_next[1]), g)
    y_to = lax.rem(jnp.where(zh == 0, c + 2, c + 6), 8)
    y_from = lax.rem(jnp.where(zh == 0, c + 6, c + 2), 8)
    has_out = jnp.where(zh == 0, y < 3, y > 0)
    has_in = jnp.where(zh == 0, y > 0, y < 3)

    def on_head(i):
        return (r, c, i)

    smalls = [
        pltpu.make_async_copy(src, dst, small_sem.at[i])
        for i, (src, dst) in enumerate([
            (x_hbm, hg.at[g]), (scale_hbm, scale_ref), (shift_hbm, shift_ref),
            (kg_hbm, kg_ref), (qg_hbm, qg_ref), (win_hbm, win_ref)])
    ]
    for copy in smalls:
        copy.start()
    w_copies = [pltpu.make_async_copy(w_hbm.at[j], wq.at[j], w_sem.at[j]) for j in range(3)]
    for j in (1, 2, 0):
        w_copies[j].start()

    def columns(i):
        return wo_hbm.at[:, pl.ds(pl.multiple_of(i * W, W), W)]

    wo_own = pltpu.make_async_copy(columns(g), wo.at[g], own_sem)
    wo_own.start()

    barrier = pltpu.get_barrier_semaphore()
    greeted = [on_head(lax.rem(g + i, NG)) for i in range(1, NG)]
    greeted += [z + (x0 + k,) for z in (z_prev, z_next) for k in range(2)]
    greeted += [(r, y_to, g), (r, y_from, g)]
    for dev in greeted:
        pl.semaphore_signal(barrier, inc=1, device_id=dev, device_id_type=MESH)
    pl.semaphore_wait(barrier, len(greeted))

    half = T // 2

    def ag_copy(slot, part, send, dev):
        piece = hg.at[slot, pl.ds(part * half, half), :]
        return pltpu.make_async_remote_copy(
            src_ref=piece, dst_ref=piece, send_sem=send, recv_sem=ag_r.at[slot, part],
            device_id=on_head(dev), device_id_type=MESH)

    gathers = []

    def gather(slot, part, send, dev):
        copy = ag_copy(slot, part, send, dev)
        copy.start()
        gathers.append(copy)

    def gathered(slot, part):
        ag_copy(slot, part, ag_s.at[0], mate).wait_recv()

    smalls[0].wait()
    for i in range(2):
        gather(g, i, ag_s.at[i], right)
        gather(g, 1 - i, ag_s.at[2 + i], left)
    for part in range(2):
        gather(g, part, ag_s.at[4 + part], mate)
    gathered(left, 0)
    gather(left, 0, agx_s.at[0], right)
    gathered(right, 1)
    gather(right, 1, agx_s.at[1], left)
    gather(left, 0, agf_s.at[0, 0], mate)
    gather(right, 1, agf_s.at[1, 1], mate)
    gathered(left, 1)
    gather(left, 1, agf_s.at[0, 1], mate)
    gathered(right, 0)
    gather(right, 0, agf_s.at[1, 0], mate)
    for part in range(2):
        gathered(peers[2], part)
        gather(peers[2], part, agf_s.at[2, part], mate)
    for dev in [mate] + [dev + 1 - 2 * core for dev in peers]:
        for part in range(2):
            gathered(dev, part)
    for copy in smalls[1:]:
        copy.wait()

    step = 32

    def norm_rows(i, _):
        rows = pl.ds(pl.multiple_of(i * step, step), step)
        parts = [hg[j, rows, :].astype(F32) for j in range(NG)]
        total = parts[0]
        for part in parts[1:]:
            total = total + part
        center = jnp.sum(total, axis=-1, keepdims=True) * (1.0 / D)
        squares = None
        for part in parts:
            off = part - center
            squares = off * off if squares is None else squares + off * off
        spread = jnp.sum(squares, axis=-1, keepdims=True) * (1.0 / D)
        inv = lax.rsqrt(spread + 1e-6)
        for j in range(NG):
            cols = slice(j * W, (j + 1) * W)
            nb[rows, cols] = (
                (parts[j] - center) * inv * (1.0 + scale_ref[:, cols]) + shift_ref[:, cols]
            ).astype(BF16)
        return 0

    lax.fori_loop(0, T // step, norm_rows, 0)

    def kv_copy(src, dst, h, part, send, dev):
        return pltpu.make_async_remote_copy(
            src_ref=kv.at[src, h, part], dst_ref=kv.at[dst, h, part],
            send_sem=send, recv_sem=kv_r.at[dst, h, part],
            device_id=dev, device_id_type=MESH)

    def own_copy(way, h, part):
        first = jnp.where(r == 0, 0, 2) if way == 0 else jnp.where(r == 3, 0, 2)
        slot = first + 3 * jnp.where(core == way, 0, 1)
        to = z_prev if way == 0 else z_next
        return kv_copy(OWN, slot, h, part, kv_s.at[way, h, part], to + (x0 + way,))

    ranks = (r, 3 - r)

    def send_own(h, part):
        for way in range(2):
            @pl.when((h == 0) | (ranks[way] > 0))
            def _():
                own_copy(way, h, part).start()

    def send_later(h):
        for way in range(2):
            @pl.when(ranks[way] == 0)
            def _():
                for part in range(2):
                    own_copy(way, h, part).start()

    def project(j):
        w_copies[j].wait()
        return jnp.dot(nb[...], wq[j], preferred_element_type=F32)

    def head_norm(values, gain):
        mean = jnp.mean(values * values, axis=-1, keepdims=True)
        return (values * lax.rsqrt(mean + 1e-6) * gain).astype(BF16)

    keys = project(1)
    for h in range(NH):
        kv[OWN, h, 0] = head_norm(keys[:, h * HD:(h + 1) * HD], kg_ref[...])
        send_own(h, 0)
    values = project(2)
    for h in range(NH):
        kv[OWN, h, 1] = values[:, h * HD:(h + 1) * HD].astype(BF16)
        send_own(h, 1)

    def q_copy(h, dev):
        return pltpu.make_async_remote_copy(
            src_ref=qs.at[0, h], dst_ref=qs.at[1, h], send_sem=q_s.at[h], recv_sem=q_r.at[h],
            device_id=(r, dev, g), device_id_type=MESH)

    def mk_copy(dev):
        return pltpu.make_async_remote_copy(
            src_ref=mk.at[0], dst_ref=mk.at[1], send_sem=mk_s, recv_sem=mk_r,
            device_id=(r, dev, g), device_id_type=MESH)

    for i in range(9):
        mk[0, i:i + 1, :] = jnp.full((1, HD), win_ref[0, 0, i].astype(F32))

    @pl.when(has_in)
    def _():
        mk_copy(y_from).start()

    queries = project(0)
    for h in range(NH):
        qs[0, h] = head_norm(queries[:, h * HD:(h + 1) * HD], qg_ref[...])

        @pl.when(has_in)
        def _():
            q_copy(h, y_from).start()

    def wo_copy(i):
        dev = lax.rem(g + i, NG)
        return pltpu.make_async_remote_copy(
            src_ref=columns(dev), dst_ref=wo.at[g], send_sem=wo_s.at[i], recv_sem=wo_r.at[g],
            device_id=on_head(dev), device_id_type=MESH)

    for i in range(1, NG):
        wo_copy(i).start()

    m_s[...] = jnp.full_like(m_s, NEG)
    l_s[...] = jnp.zeros_like(l_s)
    acc[...] = jnp.zeros_like(acc)
    block = 128

    def attend(who, slot, h, offset):
        kept = mk[who, pl.ds(offset, 1), :] > 0
        k = kv[slot, h, 0]
        v = kv[slot, h, 1]
        for i in range(T // block):
            rows = slice(i * block, (i + 1) * block)
            s = lax.dot_general(
                qs[who, h, rows, :], k, (((1,), (1,)), ((), ())), preferred_element_type=F32)
            top = jnp.max(s, axis=-1, keepdims=True) * SCALE
            old = m_s[who, h, rows, :]
            new = jnp.maximum(old, jnp.where(kept, top, NEG))
            decay = jnp.exp2(old - new)
            less = jnp.where(kept, new, -NEG)
            p = jnp.exp2(s * SCALE - jnp.concatenate([less] * (T // HD), axis=1))
            m_s[who, h, rows, :] = new
            l_s[who, h, rows, :] = l_s[who, h, rows, :] * decay + jnp.sum(p, axis=-1, keepdims=True)
            acc[who, h, rows, :] = acc[who, h, rows, :] * decay + jnp.dot(
                p.astype(BF16), v, preferred_element_type=F32)

    def own_tile(h, _):
        attend(0, OWN, h, 4)
        return 0

    lax.fori_loop(0, NH, own_tile, 0)

    def arrived(slot, h, part):
        kv_copy(OWN, slot, h, part, kv_s.at[0, h, part], (r, c, mate)).wait_recv()

    def event(at_rank, i):
        first = jnp.where(at_rank < 3, NH, 0)
        crossing = (i >= first) & (i < first + 2 * NH)
        e = jnp.where(crossing, i - first, 0)
        k = lax.rem(e, 2)
        h = jnp.where(crossing, e // 2, i)
        valid = (i >= 0) & (i < first + 2 * NH)
        return valid, crossing, k, jnp.where(valid, h, 0)

    def relay(i, part, other, act):
        valid, crossing, k, h = event(rank, i)
        near = k + 1 >= rank
        slot = jnp.where(crossing, k, 2) + 3 * other
        k_out = jnp.where(crossing, k, 1)

        @pl.when(valid & jnp.where(crossing, rank > 0, rank == 0))
        def _():
            act(kv_copy(slot, k_out + 3 * other, h, part, z_s.at[k_out, other, h, part], onward))

        @pl.when((other == 1) & valid & (near | jnp.logical_not(crossing)))
        def _():
            kind = jnp.where(crossing, k, 2)
            act(kv_copy(slot, MATE + kind, h, part, mate_s.at[kind, h, part], (r, c, mate)))

    def at_copy(slot, h, send, dev):
        return pltpu.make_async_remote_copy(
            src_ref=at.at[slot, h], dst_ref=at.at[slot, h], send_sem=send, recv_sem=at_r.at[slot, h],
            device_id=on_head(dev), device_id_type=MESH)

    def back_copies(h, dev):
        return [
            pltpu.make_async_remote_copy(
                src_ref=buf.at[0, h], dst_ref=buf.at[1, h], send_sem=back_s.at[i, h],
                recv_sem=back_r.at[i, h], device_id=(r, dev, g), device_id_type=MESH)
            for i, buf in enumerate((stats, back))
        ]

    def give_back(h):
        stats[0, h, 0:1, :] = jnp.transpose(m_s[1, h])[0:1, :]
        stats[0, h, 1:2, :] = jnp.transpose(l_s[1, h])[0:1, :]
        back[0, h] = acc[1, h].astype(BF16)
        for copy in back_copies(h, y_to):
            copy.start()

    def finish_head(h):
        @pl.when(has_in)
        def _():
            for copy in back_copies(h, y_from):
                copy.wait_recv()
            m1, l1 = [
                jnp.transpose(jnp.broadcast_to(stats[1, h, i:i + 1, :], (HD, T))) for i in range(2)]
            m0 = m_s[0, h]
            top = jnp.maximum(m0, m1)
            a0, a1 = jnp.exp2(m0 - top), jnp.exp2(m1 - top)
            l_s[0, h] = l_s[0, h] * a0 + l1 * a1
            acc[0, h] = acc[0, h] * a0 + back[1, h].astype(F32) * a1

        at[g, h] = (acc[0, h] / l_s[0, h]).astype(BF16)
        for i, dev in enumerate(peers + [mate]):
            at_copy(g, h, at_s.at[i, h], dev).start()

    def pass_head(h):
        for i, dev in enumerate(peers):
            at_copy(dev, h, at_s.at[i, h], dev).wait_recv()
            at_copy(dev, h, atf_s.at[i, h], mate).start()

    def tick(t, _):
        done = t - LAG - NH - 1

        @pl.when((t == LAG_OWN) & has_out)
        def _():
            mk_copy(y_to).wait_recv()
            for h in range(NH):
                q_copy(h, y_to).wait_recv()

        def turn_of(i, _):
            part, other = i // 2, lax.rem(i, 2)
            valid, crossing, k, h = event(rank, t)

            @pl.when(valid)
            def _():
                arrived(jnp.where(crossing, k, 2) + 3 * other, h, part)
                relay(t, part, other, lambda copy: copy.start())

            ours = lax.rem(i, 2) == 0
            far = i < 2
            at_rank = jnp.where(ours, rank, 3 - rank)
            valid, crossing, k, h = event(at_rank, t - jnp.where(ours, LAG_OWN, LAG))
            near = k + 1 >= at_rank
            downward = jnp.where(ours, core, 1 - core) == 0
            turn = jnp.where(downward, k, 3 - k) - r + 1
            kind = jnp.where(crossing, k, 2)
            slot = jnp.where(ours, kind, MATE + kind)
            side = jnp.where(far, 2 * zh, 2 - 2 * zh)
            offset = jnp.where(crossing, 3 * turn + side, jnp.where(downward, 7, 1))
            needed = valid & jnp.where(crossing, near, True)

            @pl.when(needed & (i == 1))
            def _():
                arrived(slot, h, 0)
                arrived(slot, h, 1)

            @pl.when(needed & jnp.where(far, crossing & has_out, True))
            def _():
                attend(jnp.where(far, 1, 0), slot, h, offset)

            @pl.when((i == 1) & (done >= 0) & (lax.rem(done, 2) == 0) & has_out)
            def _():
                give_back(done // 2)

            return 0

        lax.fori_loop(0, 4, turn_of, 0)

        @pl.when(t < NH - 1)
        def _():
            send_later(t + 1)

        back_in = done - LAG_BACK

        @pl.when((back_in >= 0) & (lax.rem(back_in, 2) == 0))
        def _():
            ready = back_in // 2
            finish_head(ready)

            @pl.when(ready > 0)
            def _():
                pass_head(ready - 1)

        return 0

    lax.fori_loop(0, EVENTS + LAG + LAG_BACK, tick, 0)
    pass_head(NH - 1)
    for h in range(NH):
        at_copy(mate, h, at_s.at[3, h], mate).wait_recv()
        for i, dev in enumerate(peers):
            at_copy(dev + 1 - 2 * core, h, atf_s.at[i, h], mate).wait_recv()
    wo_own.wait()
    for i in range(1, NG):
        src = lax.rem(g + i, NG)
        pltpu.make_async_remote_copy(
            src_ref=columns(src), dst_ref=wo.at[src], send_sem=wo_s.at[i], recv_sem=wo_r.at[src],
            device_id=on_head(src), device_id_type=MESH).wait_recv()


    def group(i, total):
        a = jnp.concatenate([at[i, h] for h in range(NH)], axis=1)
        part = jnp.dot(a, wo[i], preferred_element_type=F32)
        return total + part.astype(BF16).astype(F32)

    proj = lax.fori_loop(0, NG, group, jnp.zeros((T, W), F32))
    out_ref[...] = proj

    for copy in gathers:
        copy.wait_send()
    for i in range(1, NG):
        wo_copy(i).wait_send()
    for h in range(NH):
        for i, dev in enumerate(peers + [mate]):
            at_copy(g, h, at_s.at[i, h], dev).wait_send()
        for i, dev in enumerate(peers):
            at_copy(dev, h, atf_s.at[i, h], mate).wait_send()

    def sent(i, _):
        for part in range(2):
            for other in range(2):
                relay(i, part, other, lambda copy: copy.wait_send())
        return 0

    lax.fori_loop(0, EVENTS, sent, 0)

    @pl.when(has_in)
    def _():
        mk_copy(y_from).wait_send()
        for h in range(NH):
            q_copy(h, y_from).wait_send()

    @pl.when(has_out)
    def _():
        for h in range(NH):
            for copy in back_copies(h, y_to):
                copy.wait_send()

    for way in range(2):
        for h in range(NH):
            for part in range(2):
                own_copy(way, h, part).wait_send()


def on_device(
    hidden_in, mod_shift, mod_scale, mod_gate, w_qkv, query_gain, key_gain, w_out, window
):
    vmem = pl.BlockSpec(memory_space=pltpu.VMEM)
    hbm = pl.BlockSpec(memory_space=pltpu.HBM)
    dma = pltpu.SemaphoreType.DMA
    proj = pl.pallas_call(
        kernel,
        out_shape=jax.ShapeDtypeStruct((T, W), F32),
        in_specs=[hbm] * 8,
        out_specs=vmem,
        scratch_shapes=[
            pltpu.VMEM((1, D), F32),
            pltpu.VMEM((1, D), F32),
            pltpu.VMEM((1, HD), F32),
            pltpu.VMEM((1, HD), F32),
            pltpu.SMEM((1, 1, 9), jnp.int32),
            dma((6,)),
            pltpu.VMEM((NG, T, W), BF16),
            pltpu.VMEM((T, D), BF16),
            pltpu.VMEM((3, D, W), BF16),
            pltpu.VMEM((SLOTS, NH, 2, T, HD), BF16),
            pltpu.VMEM((2, NH, T, HD), BF16),
            pltpu.VMEM((2, NH, T, HD), F32),
            pltpu.VMEM((2, NH, T, HD), F32),
            pltpu.VMEM((2, NH, T, HD), F32),
            pltpu.VMEM((NG, W, W), BF16),
            pltpu.VMEM((NG, NH, T, HD), BF16),
            pltpu.VMEM((2, 16, HD), F32),
            pltpu.VMEM((2, NH, T, HD), BF16),
            pltpu.VMEM((2, NH, 8, T), F32),
            dma((3,)), dma, dma((6,)), dma((2,)), dma((3, 2)), dma((NG, 2)),
            dma((2, NH, 2)), dma((2, 2, NH, 2)), dma((3, NH, 2)), dma((SLOTS, NH, 2)),
            dma((NH,)), dma((NH,)), dma, dma, dma((2, NH)), dma((2, NH)),
            dma((NG,)), dma((NG,)), dma((4, NH)), dma((3, NH)), dma((NG, NH)),
        ],
        compiler_params=pltpu.CompilerParams(
            collective_id=0, has_side_effects=True, vmem_limit_bytes=64 * 1024 * 1024),
        cost_estimate=pl.CostEstimate(
            flops=6_000_000_000, bytes_accessed=10_000_000, transcendentals=4_000_000),
        name="tile_attention",
    )(
        hidden_in.reshape(T, W),
        mod_shift.reshape(1, D),
        mod_scale.reshape(1, D),
        jnp.transpose(w_qkv, (1, 0, 2)),
        query_gain.reshape(1, HD),
        key_gain.reshape(1, HD),
        w_out,
        window,
    )
    proj = proj.reshape(hidden_in.shape)
    return (hidden_in.astype(F32) + mod_gate * proj).astype(BF16)


def solution(mesh):
    in_specs = (
        P("row", "col", None, "head"),
        P(),
        P(),
        P("head"),
        P(None, None, "head"),
        P(),
        P(),
        P("head", None),
        P("row", "col", None),
    )
    out_specs = P("row", "col", None, "head")
    return jax.shard_map(
        on_device, mesh=mesh, in_specs=in_specs, out_specs=out_specs, check_vma=False
    )
```

time: 111 us -> 95.1 us (0.86)
  Pallas kernels: 102 us -> 92.1 us
  local copies, waits for them, and re-layouts: 7.4 us -> 0 us
  other arithmetic: 0 us -> 1.95 us
    pallas_call x1, Pallas kernels: 102 us -> 92.1 us  [on_device(): pl.pallas_call(kernel, out_shape=jax.ShapeDtypeStruct((T, W), F32), in_sp...]
    unnamed x15 -> x0, local copies, waits for them, and re-layouts: 6.72 us -> none
    convert_element_type x0 -> x1, other arithmetic: none -> 1.95 us  [on_device(): return (hidden_in.astype(F32) + mod_gate * proj).astype(BF16)]
where the time goes in v2:
time: 95.1 us; the launch traced here: 94 us
  Pallas kernels  92.1 us (97%)
  other arithmetic  1.95 us (2%)
    pallas_call x1, Pallas kernels, on_device(): pl.pallas_call(kernel, out_shape=jax.ShapeDtypeStruct((T, W), F32), in_sp...  92.1 us
    convert_element_type x1, other arithmetic, on_device(): return (hidden_in.astype(F32) + mod_gate * proj).astype(BF16)  1.95 us

profile of v2, /device:TPU:31, one launch (start us, length us, event | category | flops | bytes accessed | tf_op | source)
XLA Modules:
  0.0 94.0 jit_solution(14477365752245235021)
XLA Ops:
  0.0 92.1 %tile_attention.1 = f32[384,384]{1,0:T(8,128)} custom-call(bf16[384,384]{1,0:T(8,128)(2,1)} %bitcast.10, f32[1,3072]{1,0:T(1,128)} %bitcast.12, f32[1,3072]{1,0:T(1,128)} %bitcast.13, bf16[3,3072,384]{2,1,0:T(8,128)(2,1)} %bitcast.11, f32[1,128]{1,0:T(1,128)} %bitcast.14, f32[1,128]{1,0:T(1,128)} %bitcast.15, bf16[384,3072]{1,0:T(8,128)(2,1)} %wo_hbm.1, ...), custom_call_target="tpu_custom_call" | custom-call | flops 6000000000 | bytes 10000000 | tf_op jit(solution)/shard_map/tile_attention/pallas_call | solution.py:456
  92.1 1.9 %fusion = bf16[1,1,384,384]{3,2,1,0:T(8,128)(2,1)} fusion(f32[384,384]{1,0:T(8,128)} %tile_attention.1, bf16[1,1,384,384]{3,2,1,0:T(8,128)(2,1)} %param.9, f32[384]{0:T(512)} %param.12), kind=kLoop, calls=%fused_computation.1 | loop fusion | flops 589824 | bytes 1181184 | tf_op jit(solution)/shard_map/convert_element_type | solution.py:502

commit v3 on v2

--- a/solution.py
+++ b/solution.py
@@ -28,7 +28,8 @@
 
 
 def kernel(
-    x_hbm, shift_hbm, scale_hbm, w_hbm, qg_hbm, kg_hbm, wo_hbm, win_hbm, out_ref,
+    x_hbm, shift_hbm, scale_hbm, gate_hbm, w_hbm, qg_hbm, kg_hbm, wo_hbm, win_hbm, out_ref,
+    gate_ref, proj,
     shift_ref, scale_ref, qg_ref, kg_ref, win_ref, small_sem, hg, nb, wq, kv, qs, acc, m_s, l_s, wo, at, mk, back, stats,
     w_sem, own_sem, ag_s, agx_s, agf_s, ag_r, kv_s, z_s, mate_s, kv_r, q_s, q_r, mk_s, mk_r, back_s, back_r, wo_s, wo_r, at_s, atf_s, at_r,
 ):
@@ -58,7 +59,7 @@
         pltpu.make_async_copy(src, dst, small_sem.at[i])
         for i, (src, dst) in enumerate([
             (x_hbm, hg.at[g]), (scale_hbm, scale_ref), (shift_hbm, shift_ref),
-            (kg_hbm, kg_ref), (qg_hbm, qg_ref), (win_hbm, win_ref)])
+            (kg_hbm, kg_ref), (qg_hbm, qg_ref), (win_hbm, win_ref), (gate_hbm, gate_ref.at[0])])
     ]
     for copy in smalls:
         copy.start()
@@ -390,11 +391,6 @@
         return 0
 
     lax.fori_loop(0, EVENTS + LAG + LAG_BACK, tick, 0)
-    pass_head(NH - 1)
-    for h in range(NH):
-        at_copy(mate, h, at_s.at[3, h], mate).wait_recv()
-        for i, dev in enumerate(peers):
-            at_copy(dev + 1 - 2 * core, h, atf_s.at[i, h], mate).wait_recv()
     wo_own.wait()
     for i in range(1, NG):
         src = lax.rem(g + i, NG)
@@ -402,14 +398,33 @@
             src_ref=columns(src), dst_ref=wo.at[src], send_sem=wo_s.at[i], recv_sem=wo_r.at[src],
             device_id=on_head(src), device_id_type=MESH).wait_recv()
 
-
-    def group(i, total):
+    def group(i):
         a = jnp.concatenate([at[i, h] for h in range(NH)], axis=1)
         part = jnp.dot(a, wo[i], preferred_element_type=F32)
-        return total + part.astype(BF16).astype(F32)
-
-    proj = lax.fori_loop(0, NG, group, jnp.zeros((T, W), F32))
-    out_ref[...] = proj
+        return part.astype(BF16).astype(F32)
+
+    last = NH - 1
+    proj[...] = group(g)
+    for i, dev in enumerate(peers):
+        at_copy(dev, last, at_s.at[i, last], dev).wait_recv()
+        at_copy(dev, last, atf_s.at[i, last], mate).start()
+        if i < 2:
+            proj[...] += group(dev)
+
+    def from_mate(i, _):
+        src = mate
+        for n, dev in enumerate(peers):
+            src = jnp.where(i == n + 1, dev + 1 - 2 * core, src)
+
+        for h in range(NH):
+            at_copy(src, h, at_s.at[3, h], mate).wait_recv()
+        proj[...] += group(src)
+        return 0
+
+    from_mate(0, 0)
+    proj[...] += group(peers[2])
+    lax.fori_loop(1, 4, from_mate, 0)
+    out_ref[...] = (hg[g].astype(F32) + gate_ref[...] * proj[...]).astype(BF16)
 
     for copy in gathers:
         copy.wait_send()
@@ -453,18 +468,20 @@
     vmem = pl.BlockSpec(memory_space=pltpu.VMEM)
     hbm = pl.BlockSpec(memory_space=pltpu.HBM)
     dma = pltpu.SemaphoreType.DMA
-    proj = pl.pallas_call(
+    out = pl.pallas_call(
         kernel,
-        out_shape=jax.ShapeDtypeStruct((T, W), F32),
-        in_specs=[hbm] * 8,
+        out_shape=jax.ShapeDtypeStruct((T, W), BF16),
+        in_specs=[hbm] * 9,
         out_specs=vmem,
         scratch_shapes=[
+            pltpu.VMEM((1, W), F32),
+            pltpu.VMEM((T, W), F32),
             pltpu.VMEM((1, D), F32),
             pltpu.VMEM((1, D), F32),
             pltpu.VMEM((1, HD), F32),
             pltpu.VMEM((1, HD), F32),
             pltpu.SMEM((1, 1, 9), jnp.int32),
-            dma((6,)),
+            dma((7,)),
             pltpu.VMEM((NG, T, W), BF16),
             pltpu.VMEM((T, D), BF16),
             pltpu.VMEM((3, D, W), BF16),
@@ -492,14 +509,14 @@
         hidden_in.reshape(T, W),
         mod_shift.reshape(1, D),
         mod_scale.reshape(1, D),
+        mod_gate,
         jnp.transpose(w_qkv, (1, 0, 2)),
         query_gain.reshape(1, HD),
         key_gain.reshape(1, HD),
         w_out,
         window,
     )
-    proj = proj.reshape(hidden_in.shape)
-    return (hidden_in.astype(F32) + mod_gate * proj).astype(BF16)
+    return out.reshape(hidden_in.shape)
 
 
 def solution(mesh):

time: 95.1 us -> 91.9 us (0.966)
  Pallas kernels: 92.1 us -> 89.6 us
  other arithmetic: 1.95 us -> 0 us
  local copies, waits for them, and re-layouts: 0 us -> 1.71 us
    pallas_call x1, Pallas kernels: 92.1 us -> 89.6 us  [on_device(): pl.pallas_call(kernel, out_shape=jax.ShapeDtypeStruct((T, W), BF16), in_s...]
    convert_element_type x1 -> x0, other arithmetic: 1.95 us -> none  [on_device(): return (hidden_in.astype(F32) + mod_gate * proj).astype(BF16)]
    unnamed x0 -> x1, local copies, waits for them, and re-layouts: none -> 1.71 us
where the time goes in v3:
time: 91.9 us; the launch traced here: 91.4 us
  Pallas kernels  89.6 us (97%)
  local copies, waits for them, and re-layouts  1.71 us (2%)
    pallas_call x1, Pallas kernels, on_device(): pl.pallas_call(kernel, out_shape=jax.ShapeDtypeStruct((T, W), BF16), in_s...  89.6 us

profile of v3, /device:TPU:31, one launch (start us, length us, event | category | flops | bytes accessed | tf_op | source)
XLA Modules:
  0.0 91.4 jit_solution(1110078891938386218)
XLA Ops:
  0.0 89.6 %tile_attention.1 = bf16[384,384]{1,0:T(8,128)(2,1)} custom-call(bf16[384,384]{1,0:T(8,128)(2,1)} %bitcast.9, f32[1,3072]{1,0:T(1,128)} %bitcast.10, f32[1,3072]{1,0:T(1,128)} %bitcast.11, f32[384]{0:T(512)} %gate_hbm.1, bf16[3,3072,384]{2,1,0:T(8,128)(2,1)} %bitcast.8, f32[1,128]{1,0:T(1,128)} %bitcast.12, f32[1,128]{1,0:T(1,128)} %bitcast.13, ...), custom_call_target="tpu_custom_call" | custom-call | flops 6000000000 | bytes 10000000 | tf_op jit(solution)/shard_map/tile_attention/pallas_call | solution.py:471
  89.7 1.7 %copy.11 = bf16[1,1,384,384]{3,2,1,0:T(8,128)(2,1)} copy(bf16[1,1,384,384]{3,2,1,0:T(8,128)(2,1)} %bitcast.7) | data formatting | bytes 589824

commit v4 on v3

--- a/solution.py
+++ b/solution.py
@@ -146,7 +146,7 @@
             ).astype(BF16)
         return 0
 
-    lax.fori_loop(0, T // step, norm_rows, 0)
+    lax.fori_loop(0, T // step, norm_rows, 0, unroll=2)
 
     def kv_copy(src, dst, h, part, send, dev):
         return pltpu.make_async_remote_copy(
@@ -229,7 +229,7 @@
     m_s[...] = jnp.full_like(m_s, NEG)
     l_s[...] = jnp.zeros_like(l_s)
     acc[...] = jnp.zeros_like(acc)
-    block = 128
+    block = 384
 
     def attend(who, slot, h, offset):
         kept = mk[who, pl.ds(offset, 1), :] > 0

time: 91.9 us -> 89.7 us (0.976)
  Pallas kernels: 89.6 us -> 87.9 us
    pallas_call x1, Pallas kernels: 89.6 us -> 87.9 us  [on_device(): pl.pallas_call(kernel, out_shape=jax.ShapeDtypeStruct((T, W), BF16), in_s...]
where the time goes in v4:
time: 89.7 us; the launch traced here: 89.6 us
  Pallas kernels  87.9 us (98%)
  local copies, waits for them, and re-layouts  1.71 us (2%)
    pallas_call x1, Pallas kernels, on_device(): pl.pallas_call(kernel, out_shape=jax.ShapeDtypeStruct((T, W), BF16), in_s...  87.9 us

profile of v4, /device:TPU:31, one launch (start us, length us, event | category | flops | bytes accessed | tf_op | source)
XLA Modules:
  0.0 89.6 jit_solution(10220938100265436448)
XLA Ops:
  0.0 87.9 %tile_attention.1 = bf16[384,384]{1,0:T(8,128)(2,1)} custom-call(bf16[384,384]{1,0:T(8,128)(2,1)} %bitcast.9, f32[1,3072]{1,0:T(1,128)} %bitcast.10, f32[1,3072]{1,0:T(1,128)} %bitcast.11, f32[384]{0:T(512)} %gate_hbm.1, bf16[3,3072,384]{2,1,0:T(8,128)(2,1)} %bitcast.8, f32[1,128]{1,0:T(1,128)} %bitcast.12, f32[1,128]{1,0:T(1,128)} %bitcast.13, ...), custom_call_target="tpu_custom_call" | custom-call | flops 6000000000 | bytes 10000000 | tf_op jit(solution)/shard_map/tile_attention/pallas_call | solution.py:471
  87.9 1.7 %copy.11 = bf16[1,1,384,384]{3,2,1,0:T(8,128)(2,1)} copy(bf16[1,1,384,384]{3,2,1,0:T(8,128)(2,1)} %bitcast.7) | data formatting | bytes 589824

commit v5 on v4

--- a/solution.py
+++ b/solution.py
@@ -105,6 +105,9 @@
         gather(g, 1 - i, ag_s.at[2 + i], left)
     for part in range(2):
         gather(g, part, ag_s.at[4 + part], mate)
+    m_s[...] = jnp.full_like(m_s, NEG)
+    l_s[...] = jnp.zeros_like(l_s)
+    acc[...] = jnp.zeros_like(acc)
     gathered(left, 0)
     gather(left, 0, agx_s.at[0], right)
     gathered(right, 1)
@@ -226,9 +229,6 @@
     for i in range(1, NG):
         wo_copy(i).start()
 
-    m_s[...] = jnp.full_like(m_s, NEG)
-    l_s[...] = jnp.zeros_like(l_s)
-    acc[...] = jnp.zeros_like(acc)
     block = 384
 
     def attend(who, slot, h, offset):

time: 89.7 us -> 89.7 us (level)
  no operation moved by 1% of the time
where the time goes in v5:
time: 89.7 us; the launch traced here: 89.6 us
  Pallas kernels  87.9 us (98%)
  local copies, waits for them, and re-layouts  1.71 us (2%)
    pallas_call x1, Pallas kernels, on_device(): pl.pallas_call(kernel, out_shape=jax.ShapeDtypeStruct((T, W), BF16), in_s...  87.9 us

profile of v5, /device:TPU:31, one launch (start us, length us, event | category | flops | bytes accessed | tf_op | source)
XLA Modules:
  0.0 89.6 jit_solution(18244693048257675343)
XLA Ops:
  0.0 87.9 %tile_attention.1 = bf16[384,384]{1,0:T(8,128)(2,1)} custom-call(bf16[384,384]{1,0:T(8,128)(2,1)} %bitcast.9, f32[1,3072]{1,0:T(1,128)} %bitcast.10, f32[1,3072]{1,0:T(1,128)} %bitcast.11, f32[384]{0:T(512)} %gate_hbm.1, bf16[3,3072,384]{2,1,0:T(8,128)(2,1)} %bitcast.8, f32[1,128]{1,0:T(1,128)} %bitcast.12, f32[1,128]{1,0:T(1,128)} %bitcast.13, ...), custom_call_target="tpu_custom_call" | custom-call | flops 6000000000 | bytes 10000000 | tf_op jit(solution)/shard_map/tile_attention/pallas_call | solution.py:471
  87.9 1.7 %copy.11 = bf16[1,1,384,384]{3,2,1,0:T(8,128)(2,1)} copy(bf16[1,1,384,384]{3,2,1,0:T(8,128)(2,1)} %bitcast.7) | data formatting | bytes 589824
